TPU v7x, 32 devices: a whole 2x2x4 slice. The times are simulated.
32 devices in a mesh: expert: 8 (over z, x), tensor: 4 (over y, core).
Axes of the slice: x: 2, y: 2, z: 4, core: 2. Of those that a mesh axis runs over, the one named last changes fastest.
Arguments:
- tokens: bfloat16 [2, 1024, 768], P(None, 'expert'), may hold values from -6 to 6
- out_grad: bfloat16 [2, 1024, 768], P(None, 'expert'), may hold values from -6 to 6
- routes: int32 [2, 1024, 2], P(None, 'expert'), may hold values from 0 to 7, as said below
- lengths: int32 [2, 7], replicated, may hold values from 1 to 512, 1024 in all within a row
- parents: int32 [2, 7], replicated, may hold values from 0 to 5, as said below
- attn_gain: bfloat16 [768], P('expert'), may hold values from 0.5 to 1.5
- ffn_gain: bfloat16 [768], P('expert'), may hold values from 0.5 to 1.5
- w_query: bfloat16 [768, 768], P('expert', 'tensor'), may hold values from -0.21875 to 0.21875
- w_key: bfloat16 [768, 768], P('expert', 'tensor'), may hold values from -0.21875 to 0.21875
- w_value: bfloat16 [768, 768], P('expert', 'tensor'), may hold values from -0.21875 to 0.21875
- w_out: bfloat16 [768, 768], P('tensor', 'expert'), may hold values from -0.875 to 0.875
- router: bfloat16 [768, 8], P('expert'), may hold values from -0.15625 to 0.15625
- shared_gate: bfloat16 [768, 2048], P('expert', 'tensor'), may hold values from -0.21875 to 0.21875
- shared_up: bfloat16 [768, 2048], P('expert', 'tensor'), may hold values from -0.21875 to 0.21875
- shared_down: bfloat16 [2048, 768], P('tensor', 'expert'), may hold values from -0.125 to 0.125
- expert_gate: bfloat16 [8, 768, 2048], P('expert', None, 'tensor'), may hold values from -0.21875 to 0.21875
- expert_up: bfloat16 [8, 768, 2048], P('expert', None, 'tensor'), may hold values from -0.21875 to 0.21875
- expert_down: bfloat16 [8, 2048, 768], P('expert', 'tensor'), may hold values from -0.125 to 0.125
Outputs:
- out: bfloat16 [2, 1024, 768], P(None, 'expert')
- grad_tokens: float32 [2, 1024, 768], P(None, 'expert')
- grad_attn_gain: float32 [768], P('expert')
- grad_ffn_gain: float32 [768], P('expert')
- grad_w_query: float32 [768, 768], P('expert', 'tensor')
- grad_w_key: float32 [768, 768], P('expert', 'tensor')
- grad_w_value: float32 [768, 768], P('expert', 'tensor')
- grad_w_out: float32 [768, 768], P('tensor', 'expert')
- grad_router: float32 [768, 8], P('expert')
- grad_shared_gate: float32 [768, 2048], P('expert', 'tensor')
- grad_shared_up: float32 [768, 2048], P('expert', 'tensor')
- grad_shared_down: float32 [2048, 768], P('tensor', 'expert')
- grad_expert_gate: float32 [8, 768, 2048], P('expert', None, 'tensor')
- grad_expert_up: float32 [8, 768, 2048], P('expert', None, 'tensor')
- grad_expert_down: float32 [8, 2048, 768], P('expert', 'tensor')
Inputs may be any that keep to these rules, and one draw needn't show every extreme that they name: In each aligned block of 128 rows of routes (the rows of one device in one micro-batch) the two experts of a token differ, no expert is named more than 64 times, and some expert is named exactly 64 times in every block. parents[m, s] < s for s >= 1 and parents[m, 0] = 0, so every path ends at segment 0; the last segment's parent is segment 7 - 2.
All inputs are finite; a program needn't handle non-finite values.
Results may differ from a plain program's by a relative error of at most 0.017.
Values may be sent and summed in bfloat16 or wider, within the bound.
A program may use at most 192 MiB of HBM per device.

v0:
```python
import functools
import math
import types

import jax
import jax.numpy as jnp
from jax import lax
from jax.experimental import pallas as pl
from jax.experimental.pallas import tpu as pltpu
from jax.sharding import PartitionSpec as P

HEAD = 64


EPSILON = 1e-06
ROPE_BASE = 10000.0
KEY_BLOCK = 2048


def matmul(left, right):
    return jnp.dot(left, right, preferred_element_type=jnp.float32)


def tree_tables(lengths, parents):
    seg_count = lengths.shape[0]
    identity = jnp.arange(seg_count, dtype=jnp.int32)
    current = identity
    ancestry = jnp.zeros((seg_count, seg_count), jnp.float32)
    for depth_level in range(seg_count):
        chosen_mask = current[:, None] == identity[None, :]
        ancestry = jnp.maximum(ancestry, chosen_mask.astype(jnp.float32))
        current = jnp.sum(jnp.where(chosen_mask, parents[None, :], 0), axis=1)
    seg_ends = jnp.cumsum(lengths)
    starts = seg_ends - lengths
    sizes_float = lengths.astype(jnp.float32)
    offsets = jnp.sum(ancestry * sizes_float[None, :], axis=1) - sizes_float
    return (ancestry, starts, seg_ends, offsets)


def row_tables(row_ids, starts, seg_ends, offsets):
    member = (
        (row_ids[:, None] >= starts[None, :]) & (row_ids[:, None] < seg_ends[None, :])
    ).astype(jnp.float32)
    position_shift = offsets - starts.astype(jnp.float32)
    position = jnp.sum(member * position_shift[None, :], axis=1) + row_ids.astype(jnp.float32)
    return (member, position)


def rotary_tables(position, half_width):
    frequency = ROPE_BASE ** (-jnp.arange(half_width, dtype=jnp.float32) / half_width)
    angles = position[:, None] * frequency[None, :]
    return (jnp.cos(angles)[:, None, :], jnp.sin(angles)[:, None, :])


def rotate(head_values, position):
    half_width = head_values.shape[-1] // 2
    cosines, sine_values = rotary_tables(position, half_width)
    first_half = head_values[..., :half_width]
    second_half = head_values[..., half_width:]
    return jnp.concatenate(
        [
            first_half * cosines - second_half * sine_values,
            second_half * cosines + first_half * sine_values,
        ],
        axis=-1,
    )


def rotate_back(grad_heads, position):
    half_width = grad_heads.shape[-1] // 2
    cosines, sine_values = rotary_tables(position, half_width)
    first_half = grad_heads[..., :half_width]
    second_half = grad_heads[..., half_width:]
    return jnp.concatenate(
        [
            first_half * cosines + second_half * sine_values,
            second_half * cosines - first_half * sine_values,
        ],
        axis=-1,
    )


def silu_parts(gate_val):
    sigmoid_val = jax.nn.sigmoid(gate_val)
    return (gate_val * sigmoid_val, sigmoid_val * (1.0 + gate_val * (1.0 - sigmoid_val)))


def rms_back(grad_normed, source, norm_scale, gain):
    weighted = grad_normed * gain
    inner_mean = jnp.mean(weighted * source, axis=1, keepdims=True)
    return (
        norm_scale * weighted - norm_scale**3 * source * inner_mean,
        jnp.sum(grad_normed * source * norm_scale, axis=0),
    )


def visible(reach_rows, query_ids, key_member, key_ids):
    linked = matmul(reach_rows, key_member.T) > 0.5
    return linked & (key_ids[None, :] <= query_ids[:, None])


def score_block(query_heads, key_heads, seen, score_scale):
    scores = (
        jnp.einsum("qhd,khd->hqk", query_heads, key_heads, preferred_element_type=jnp.float32)
        * score_scale
    )
    return jnp.where(seen[None], jnp.exp(scores), 0.0)


def score_grads(weights_exp, grad_summed, value_heads, delta_rows):
    grad_exp = jnp.einsum(
        "qhd,khd->hqk", grad_summed, value_heads, preferred_element_type=jnp.float32
    )
    return (weights_exp * (grad_exp - jnp.transpose(delta_rows)[:, :, None])).astype(jnp.bfloat16)


def plain_body(
    tokens,
    out_grad,
    routes,
    lengths,
    parents,
    attn_gain,
    ffn_gain,
    w_query,
    w_key,
    w_value,
    w_out,
    router,
    shared_gate,
    shared_up,
    shared_down,
    expert_gate,
    expert_up,
    expert_down,
):
    micro_count, row_count, model_width = tokens.shape
    devices = lax.axis_size("expert")
    tree_rows = row_count * devices
    expert_count = router.shape[1]
    owners = devices // expert_count
    capacity = 4 * row_count // expert_count
    score_scale = HEAD ** (-0.5)
    local_rows = lax.axis_index("expert") * row_count + jnp.arange(row_count, dtype=jnp.int32)
    part_gate = expert_gate[0]
    part_up = expert_up[0]
    part_down = expert_down[0]
    labels = jnp.arange(expert_count, dtype=jnp.int32)
    slot_ids = jnp.arange(expert_count * capacity, dtype=jnp.int32)
    pair_ids = jnp.arange(2 * row_count, dtype=jnp.int32)
    block_size = math.gcd(tree_rows, KEY_BLOCK)
    block_count = tree_rows // block_size
    layer_outputs = []
    token_gradients = []
    dense_sums = None
    expert_sums = None
    for micro_step in range(micro_count):
        gathered = (
            lax.all_gather(attn_gain, "expert", axis=0, tiled=True),
            lax.all_gather(ffn_gain, "expert", axis=0, tiled=True),
            lax.all_gather(w_query, "expert", axis=0, tiled=True),
            lax.all_gather(w_key, "expert", axis=0, tiled=True),
            lax.all_gather(w_value, "expert", axis=0, tiled=True),
            lax.all_gather(w_out, "expert", axis=1, tiled=True),
            lax.all_gather(router, "expert", axis=0, tiled=True),
            lax.all_gather(shared_gate, "expert", axis=0, tiled=True),
            lax.all_gather(shared_up, "expert", axis=0, tiled=True),
            lax.all_gather(shared_down, "expert", axis=1, tiled=True),
        )
        (
            gain_one,
            gain_two,
            query_weight,
            key_weight,
            value_weight,
            out_weight,
            router_weight,
            gate_weight,
            up_weight,
            down_weight,
        ) = gathered
        local_width = query_weight.shape[1]
        head_count = local_width // HEAD
        ancestry, starts, seg_ends, offsets = tree_tables(lengths[micro_step], parents[micro_step])
        member, position = row_tables(local_rows, starts, seg_ends, offsets)
        reach = matmul(member, ancestry)
        tokens_now = tokens[micro_step].astype(jnp.float32)
        norm_one = lax.rsqrt(jnp.mean(tokens_now * tokens_now, axis=1, keepdims=True) + EPSILON)
        normed_one = (tokens_now * norm_one * gain_one).astype(jnp.bfloat16)
        query_pre = matmul(normed_one, query_weight).reshape(row_count, head_count, HEAD)
        key_pre = matmul(normed_one, key_weight).reshape(row_count, head_count, HEAD)
        value_low = matmul(normed_one, value_weight).astype(jnp.bfloat16)
        queries = rotate(query_pre, position).astype(jnp.bfloat16)
        key_heads = rotate(key_pre, position).astype(jnp.bfloat16)
        key_value = jnp.concatenate([key_heads.reshape(row_count, local_width), value_low], axis=1)
        all_pairs = lax.all_gather(key_value, "expert", axis=0, tiled=True)

        def key_block_parts(block_index):
            first_key = block_index * block_size
            key_block = lax.dynamic_slice_in_dim(all_pairs, first_key, block_size, 0)
            key_ids = first_key + jnp.arange(block_size, dtype=jnp.int32)
            key_member, unused = row_tables(key_ids, starts, seg_ends, offsets)
            seen = visible(reach, local_rows, key_member, key_ids)
            block_keys = key_block[:, :local_width].reshape(block_size, head_count, HEAD)
            block_values = key_block[:, local_width:].reshape(block_size, head_count, HEAD)
            return (seen, block_keys, block_values)

        def forward_step(block_index, totals):
            seen, block_keys, block_values = key_block_parts(block_index)
            weights_exp = score_block(queries, block_keys, seen, score_scale)
            summed_part = jnp.einsum(
                "hqk,khd->qhd",
                weights_exp.astype(jnp.bfloat16),
                block_values,
                preferred_element_type=jnp.float32,
            )
            return (
                totals[0] + summed_part.reshape(row_count, local_width),
                totals[1] + jnp.transpose(jnp.sum(weights_exp, axis=2)),
            )

        initial = (
            jnp.zeros((row_count, local_width), jnp.float32),
            jnp.zeros((row_count, head_count), jnp.float32),
        )
        summed, row_total = lax.fori_loop(0, block_count, forward_step, initial)
        mixed = summed.reshape(row_count, head_count, HEAD) / row_total[:, :, None]
        mixed_low = mixed.reshape(row_count, local_width).astype(jnp.bfloat16)
        attn_out = lax.psum(matmul(mixed_low, out_weight), "tensor")
        residual = tokens_now + attn_out
        norm_two = lax.rsqrt(jnp.mean(residual * residual, axis=1, keepdims=True) + EPSILON)
        normed_two = (residual * norm_two * gain_two).astype(jnp.bfloat16)
        shared_g = matmul(normed_two, gate_weight)
        shared_u = matmul(normed_two, up_weight)
        shared_act, shared_slope = silu_parts(shared_g)
        shared_h = (shared_act * shared_u).astype(jnp.bfloat16)
        shared_y = matmul(shared_h, down_weight)
        logits = matmul(normed_two, router_weight)
        route_now = routes[micro_step]
        choose = (route_now[:, :, None] == labels[None, None, :]).astype(jnp.float32)
        gate_values = jax.nn.softmax(jnp.sum(choose * logits[:, None, :], axis=2), axis=1)
        flat_routes = route_now.reshape(2 * row_count)
        expert_hits = (flat_routes[:, None] == labels[None, :]).astype(jnp.int32)
        slot_rank = jnp.sum((jnp.cumsum(expert_hits, axis=0) - expert_hits) * expert_hits, axis=1)
        slot_index = flat_routes * capacity + slot_rank
        slot_match = slot_index[None, :] == slot_ids[:, None]
        filled = jnp.any(slot_match, axis=1)
        source = jnp.sum(jnp.where(slot_match, pair_ids[None, :], 0), axis=1)

        def to_owners(table, row_index):
            picked = jnp.take(table, row_index, axis=0)
            picked = jnp.where(filled[:, None], picked, jnp.zeros_like(picked))
            spread = jnp.broadcast_to(
                picked.reshape(expert_count, 1, capacity, model_width),
                (expert_count, owners, capacity, model_width),
            )
            return spread.reshape(devices, capacity, model_width)

        def from_owners(returned):
            merged = jnp.sum(
                returned.reshape(expert_count, owners, capacity, model_width), axis=1
            ).reshape(expert_count * capacity, model_width)
            return jnp.take(merged, slot_index, axis=0).reshape(row_count, 2, model_width)

        arrived = lax.all_to_all(
            to_owners(normed_two, source // 2), "expert", split_axis=0, concat_axis=0, tiled=True
        )
        slot_count = arrived.shape[1]
        flat_in = arrived.reshape(devices * slot_count, model_width)
        expert_g = matmul(flat_in, part_gate)
        expert_u = matmul(flat_in, part_up)
        expert_act, expert_unused = silu_parts(expert_g)
        expert_h = (expert_act * expert_u).astype(jnp.bfloat16)
        partial_out = matmul(expert_h, part_down).reshape(devices, slot_count, model_width)
        combined = lax.all_to_all(
            partial_out.astype(jnp.bfloat16), "expert", split_axis=0, concat_axis=0, tiled=True
        ).astype(partial_out.dtype)
        hidden_width = expert_g.shape[1]
        combined, arrived, kept_g, kept_u, kept_h = (
            combined,
            arrived,
            expert_g.reshape(devices, slot_count, hidden_width),
            expert_u.reshape(devices, slot_count, hidden_width),
            expert_h.reshape(devices, slot_count, hidden_width),
        )
        expert_y = from_owners(combined)
        cot_low = out_grad[micro_step]
        cotangent = cot_low.astype(jnp.float32)
        moe_part = jnp.sum(gate_values[:, :, None] * expert_y, axis=1)
        gate_dots = jnp.sum(cotangent[:, None, :] * expert_y, axis=2)
        ffn_out, grad_gate = (
            lax.psum((shared_y + moe_part).astype(jnp.bfloat16), "tensor").astype(jnp.float32),
            lax.psum(gate_dots.astype(jnp.bfloat16), "tensor").astype(jnp.float32),
        )
        layer_outputs.append((residual + ffn_out).astype(jnp.bfloat16))
        grad_shared_h = matmul(cot_low, down_weight.T)
        grad_shared_g = (grad_shared_h * shared_u * shared_slope).astype(jnp.bfloat16)
        grad_shared_u = (grad_shared_h * shared_act).astype(jnp.bfloat16)
        grad_chosen = gate_values * (
            grad_gate - jnp.sum(gate_values * grad_gate, axis=1, keepdims=True)
        )
        grad_logits = jnp.sum(choose * grad_chosen[:, :, None], axis=1).astype(jnp.bfloat16)
        grad_pairs_out = (
            (gate_values[:, :, None] * cotangent[:, None, :])
            .astype(jnp.bfloat16)
            .reshape(2 * row_count, model_width)
        )
        arrived_grad = lax.all_to_all(
            to_owners(grad_pairs_out, source), "expert", split_axis=0, concat_axis=0, tiled=True
        )
        slot_total = arrived_grad.shape[0] * arrived_grad.shape[1]
        flat_grad = arrived_grad.reshape(slot_total, model_width)
        flat_in = arrived.reshape(slot_total, model_width)
        hidden_width = kept_g.shape[2]
        expert_g = kept_g.reshape(slot_total, hidden_width)
        expert_u = kept_u.reshape(slot_total, hidden_width)
        expert_h = kept_h.reshape(slot_total, hidden_width)
        expert_act, expert_slope = silu_parts(expert_g)
        grad_hidden = matmul(flat_grad, part_down.T)
        grad_expert_g = (grad_hidden * expert_u * expert_slope).astype(jnp.bfloat16)
        grad_expert_u = (grad_hidden * expert_act).astype(jnp.bfloat16)
        grad_in = matmul(grad_expert_g, part_gate.T) + matmul(grad_expert_u, part_up.T)
        returned = lax.all_to_all(
            grad_in.reshape(arrived_grad.shape[0], arrived_grad.shape[1], model_width),
            "expert",
            split_axis=0,
            concat_axis=0,
            tiled=True,
        )
        normed_part = (
            matmul(grad_shared_g, gate_weight.T)
            + matmul(grad_shared_u, up_weight.T)
            + jnp.sum(from_owners(returned), axis=1)
        )
        grad_normed_two = lax.psum(normed_part, "tensor") + matmul(grad_logits, router_weight.T)
        grad_norm_part, grad_gain_two = rms_back(grad_normed_two, residual, norm_two, gain_two)
        grad_residual = cotangent + grad_norm_part
        grad_attn = grad_residual.astype(jnp.bfloat16)
        grad_mixed = matmul(grad_attn, out_weight.T).reshape(row_count, head_count, HEAD)
        grad_summed = (grad_mixed / row_total[:, :, None]).astype(jnp.bfloat16)
        delta_rows = jnp.sum(grad_mixed * mixed, axis=2) / row_total

        def block_terms(block_index):
            seen, block_keys, block_values = key_block_parts(block_index)
            weights_exp = score_block(queries, block_keys, seen, score_scale)
            grad_scores = score_grads(weights_exp, grad_summed, block_values, delta_rows)
            return (weights_exp, grad_scores, block_keys)

        zero_query = jnp.zeros((row_count, head_count, HEAD), jnp.float32)

        def key_step(gradient_query_weight, block_index):
            weights_exp, grad_scores, block_keys = block_terms(block_index)
            gradient_query_weight = (
                gradient_query_weight
                + jnp.einsum(
                    "hqk,khd->qhd", grad_scores, block_keys, preferred_element_type=jnp.float32
                )
                * score_scale
            )
            grad_keys = (
                jnp.einsum("hqk,qhd->khd", grad_scores, queries, preferred_element_type=jnp.float32)
                * score_scale
            )
            grad_values = jnp.einsum(
                "hqk,qhd->khd",
                weights_exp.astype(jnp.bfloat16),
                grad_summed,
                preferred_element_type=jnp.float32,
            )
            return (
                gradient_query_weight,
                jnp.concatenate(
                    [
                        grad_keys.reshape(block_size, local_width),
                        grad_values.reshape(block_size, local_width),
                    ],
                    axis=1,
                ),
            )

        gradient_query_weight, key_terms = lax.scan(
            key_step, zero_query, jnp.arange(block_count, dtype=jnp.int32)
        )
        grad_pairs = lax.psum_scatter(
            key_terms.reshape(tree_rows, 2 * local_width), "expert", scatter_dimension=0, tiled=True
        )
        grad_keys_rot = grad_pairs[:, :local_width].reshape(row_count, head_count, HEAD)
        grad_query_pre = (
            rotate_back(gradient_query_weight, position)
            .reshape(row_count, local_width)
            .astype(jnp.bfloat16)
        )
        grad_key_pre = (
            rotate_back(grad_keys_rot, position)
            .reshape(row_count, local_width)
            .astype(jnp.bfloat16)
        )
        grad_value_low = grad_pairs[:, local_width:].astype(jnp.bfloat16)
        normed_grad = (
            matmul(grad_query_pre, query_weight.T)
            + matmul(grad_key_pre, key_weight.T)
            + matmul(grad_value_low, value_weight.T)
        )
        grad_normed_one = lax.psum(normed_grad.astype(jnp.bfloat16), "tensor").astype(jnp.float32)
        grad_norm_first, grad_gain_one = rms_back(grad_normed_one, tokens_now, norm_one, gain_one)
        token_gradients.append(grad_residual + grad_norm_first)
        dense_step = (
            grad_gain_one,
            grad_gain_two,
            matmul(normed_one.T, grad_query_pre),
            matmul(normed_one.T, grad_key_pre),
            matmul(normed_one.T, grad_value_low),
            matmul(mixed_low.T, grad_attn),
            matmul(normed_two.T, grad_logits),
            matmul(normed_two.T, grad_shared_g),
            matmul(normed_two.T, grad_shared_u),
            matmul(shared_h.T, cot_low),
        )
        expert_step = (
            matmul(flat_in.T, grad_expert_g),
            matmul(flat_in.T, grad_expert_u),
            matmul(expert_h.T, flat_grad),
        )
        if dense_sums is None:
            dense_sums = dense_step
            expert_sums = expert_step
        else:
            dense_sums = tuple(
                (earlier + latest for earlier, latest in zip(dense_sums, dense_step))
            )
            expert_sums = tuple(
                (earlier + latest for earlier, latest in zip(expert_sums, expert_step))
            )
    final_gate, final_up, final_down = expert_sums
    reduced = (
        lax.psum_scatter(dense_sums[0], "expert", scatter_dimension=0, tiled=True),
        lax.psum_scatter(dense_sums[1], "expert", scatter_dimension=0, tiled=True),
        lax.psum_scatter(dense_sums[2], "expert", scatter_dimension=0, tiled=True),
        lax.psum_scatter(dense_sums[3], "expert", scatter_dimension=0, tiled=True),
        lax.psum_scatter(dense_sums[4], "expert", scatter_dimension=0, tiled=True),
        lax.psum_scatter(dense_sums[5], "expert", scatter_dimension=1, tiled=True),
        lax.psum_scatter(dense_sums[6], "expert", scatter_dimension=0, tiled=True),
        lax.psum_scatter(dense_sums[7], "expert", scatter_dimension=0, tiled=True),
        lax.psum_scatter(dense_sums[8], "expert", scatter_dimension=0, tiled=True),
        lax.psum_scatter(dense_sums[9], "expert", scatter_dimension=1, tiled=True),
    )
    return (
        jnp.stack(layer_outputs),
        jnp.stack(token_gradients),
        reduced[0],
        reduced[1],
        reduced[2],
        reduced[3],
        reduced[4],
        reduced[5],
        reduced[6],
        reduced[7],
        reduced[8],
        reduced[9],
        final_gate[None],
        final_up[None],
        final_down[None],
    )


MESH = pl.DeviceIdType.MESH
BF = jnp.bfloat16
F32 = jnp.float32
EXACT = lax.Precision.HIGHEST
VMEM_LIMIT = 63 * 2**20


def product(left, right, dims, precision=None):
    return lax.dot_general(
        left, right, (dims, ((), ())), preferred_element_type=F32, precision=precision
    )


def dot(left, right, precision=None):
    return product(left, right, ((1,), (0,)), precision)


def dot_nt(left, right, precision=None):
    return product(left, right, ((1,), (1,)), precision)


def dot_tn(left, right, precision=None):
    return product(left, right, ((0,), (0,)), precision)


def iota(shape, dim):
    return lax.broadcasted_iota(jnp.int32, shape, dim)


class Net:
    def __init__(self, expert_size, send_sems, recv_sems):
        self.e = lax.axis_index("expert")
        self.t = lax.axis_index("tensor")
        self.n = expert_size
        self.nz = expert_size // 2
        self.z = self.e // 2
        self.x = self.e % 2
        self.y = self.t // 2
        self.core = self.t % 2
        self.send_sems = send_sems
        self.recv_sems = recv_sems
        self.sends = 0
        self.free = []
        self.recvs = 0
        self.open = []

    def recv_slots(self, count):
        first = self.recvs
        self.recvs += count
        return first

    def ids(self, to):
        return {"expert": to[0], "tensor": to[1]}

    def send_slot(self):
        if not self.free:
            self.free.append(self.sends)
            self.sends += 1
        return self.free.pop(0)

    def push(self, src, dst, to, slot, when=None, bulk=False, shared=None):
        send = self.send_slot() if shared is None else shared
        copy = pltpu.make_async_remote_copy(
            src_ref=src,
            dst_ref=dst,
            send_sem=self.send_sems.at[send],
            recv_sem=self.recv_sems.at[slot],
            device_id=self.ids(to),
            device_id_type=MESH,
        )
        if when is None:
            copy.start()
        else:
            pl.when(when)(copy.start)
        if shared is None:
            self.open.append((copy, when, send, bulk))

    def all_sent(self, part, send):
        copy = pltpu.make_async_remote_copy(
            src_ref=part,
            dst_ref=part,
            send_sem=self.send_sems.at[send],
            recv_sem=self.recv_sems.at[0],
            device_id=self.ids(self.other_core()),
            device_id_type=MESH,
        )
        self.open.append((copy, None, send, False))

    def landed(self, dst, slot, when=None):
        copy = pltpu.make_async_remote_copy(
            src_ref=dst,
            dst_ref=dst,
            send_sem=self.send_sems.at[0],
            recv_sem=self.recv_sems.at[slot],
            device_id=self.ids(self.other_core()),
            device_id_type=MESH,
        )
        if when is None:
            copy.wait_recv()
        else:
            pl.when(when)(copy.wait_recv)

    def drain(self, bulk=True):
        for copy, when, send, is_bulk in self.open:
            if bulk or not is_bulk:
                if when is None:
                    copy.wait_send()
                else:
                    pl.when(when)(copy.wait_send)
                self.free.append(send)
        self.open = [one for one in self.open if one[3] and not bulk]

    def other_core(self):
        return (self.e, self.t + 1 - 2 * self.core)

    def across_y(self):
        return (self.e, (self.t + 2) % 4)

    def across_x(self):
        return (self.e + 1 - 2 * self.x, self.t)

    def peer(self, step):
        return (self.e + step) % self.n

    def greet(self):
        barrier = pltpu.get_barrier_semaphore()
        partners = [(self.peer(d), self.t) for d in range(1, self.n)]
        partners += [self.other_core(), self.across_y()]
        for to in partners:
            pl.semaphore_signal(barrier, inc=1, device_id=self.ids(to), device_id_type=MESH)
        return lambda: pl.semaphore_wait(barrier, len(partners))


class Gather:
    def __init__(self, net, block, chunks=1, on_land=None):
        self.net, self.block, self.chunks, self.on_land = net, block, chunks, on_land
        self.slot = net.recv_slots(net.n * chunks)

    def start(self):
        net = self.net
        for k in range(self.chunks):
            own, slot = self.block(net.e, k), self.slot + net.e * self.chunks + k
            for way in (1, -1):
                there = net.z + way
                fits_in = (there >= 0) & (there < net.nz)
                net.push(own, own, (there % net.nz * 2 + net.x, net.t), slot, fits_in)
            net.push(own, own, net.across_x(), slot)

    def step(self, distance):
        net = self.net
        for k in range(self.chunks):
            for way in (1, -1):
                source, there = net.z - way * distance, net.z + way
                real = (source >= 0) & (source < net.nz)
                onward = real & (there >= 0) & (there < net.nz)
                b = source % net.nz * 2 + net.x
                part, slot = self.block(b, k), self.slot + b * self.chunks + k
                net.landed(part, slot, real)
                net.push(part, part, (there % net.nz * 2 + net.x, net.t), slot, onward)
                net.push(part, part, net.across_x(), slot, real)
                if self.on_land is not None:
                    self.on_land(b, real)

    def land(self, b):
        net = self.net
        for k in range(self.chunks):
            net.landed(self.block(b, k), self.slot + b * self.chunks + k)
        if self.on_land is not None:
            self.on_land(b, None)

    def finish(self):
        for d in range(self.net.nz):
            self.land((self.net.z + d) % self.net.nz * 2 + 1 - self.net.x)


class Scatter:
    def __init__(self, net, block, from_x, from_z):
        self.net, self.block = net, block
        self.from_x, self.from_z = from_x, from_z
        self.slot_x = net.recv_slots(net.nz)
        self.slot_z = net.recv_slots(net.nz)

    def start(self):
        net = self.net
        for d in range(1, net.nz + 1):
            zz = (net.z + d) % net.nz
            net.push(
                self.block(zz * 2 + 1 - net.x),
                self.from_x.at[zz],
                net.across_x(),
                self.slot_x + zz,
                bulk=True,
            )

    def forward(self):
        net = self.net
        for d in range(1, net.nz):
            zz = (net.z + d) % net.nz
            net.landed(self.from_x.at[zz], self.slot_x + zz)
            pair = self.block(zz * 2 + net.x)[...].astype(F32) + self.from_x[zz].astype(F32)
            self.from_x[zz] = pair.astype(BF)
            net.push(
                self.from_x.at[zz],
                self.from_z.at[net.z],
                (zz * 2 + net.x, net.t),
                self.slot_z + net.z,
            )

    def finish(self):
        net = self.net
        net.landed(self.from_x.at[net.z], self.slot_x + net.z)
        total = self.block(net.e)[...].astype(F32) + self.from_x[net.z].astype(F32)
        for d in range(1, net.nz):
            zz = (net.z + d) % net.nz
            net.landed(self.from_z.at[zz], self.slot_z + zz)
            total = total + self.from_z[zz].astype(F32)
        return total


class Chain:
    def __init__(self, net, block, from_x, from_z):
        self.net, self.block = net, block
        self.from_x, self.from_z = from_x, from_z
        self.slot_x = net.recv_slots(net.nz)
        self.slot_z = net.recv_slots(net.nz + 1)

    def start(self):
        net = self.net
        high = net.z // 2
        for zz in (3 - 3 * high, 2 - high, 1 - net.z + 4 * high, net.z):
            net.push(
                self.block(zz * 2 + 1 - net.x),
                self.from_x.at[zz],
                net.across_x(),
                self.slot_x + zz,
                bulk=True,
            )

    def place(self, way, zz, holder):
        return zz if way == 1 else zz + (zz == holder).astype(jnp.int32) * (self.net.nz - zz)

    def step(self, distance):
        net = self.net
        for way in (1, -1):
            target, before = net.z + way * distance, net.z - way
            real = (target >= 0) & (target < net.nz)
            fed = real & (before >= 0) & (before < net.nz)
            zz = target % net.nz
            there = (net.z + way) % net.nz
            here = self.place(way, zz, net.z)
            onward = self.place(way, zz, there)

            @pl.when(real)
            def _():
                net.landed(self.from_x.at[zz], self.slot_x + zz)

            @pl.when(fed)
            def _():
                net.landed(self.from_z.at[here], self.slot_z + here)
                both = self.from_x[zz].astype(F32) + self.from_z[here].astype(F32)
                self.from_x[zz] = (both + self.block(zz * 2 + net.x)[...].astype(F32)).astype(BF)

            @pl.when(real & ~fed)
            def _():
                own = self.block(zz * 2 + net.x)[...].astype(F32)
                self.from_x[zz] = (self.from_x[zz].astype(F32) + own).astype(BF)

            net.push(
                self.from_x.at[zz],
                self.from_z.at[onward],
                (there * 2 + net.x, net.t),
                self.slot_z + onward,
                when=real,
                bulk=True,
            )

    def finish(self, target):
        net = self.net
        net.landed(self.from_x.at[net.z], self.slot_x + net.z)
        target[...] = self.block(net.e)[...].astype(F32) + self.from_x[net.z].astype(F32)
        for way in (1, -1):
            before = net.z - way
            here = self.place(way, net.z, net.z)

            @pl.when((before >= 0) & (before < net.nz))
            def _():
                net.landed(self.from_z.at[here], self.slot_z + here)
                target[...] += self.from_z[here].astype(F32)


class Exchange:
    def __init__(self, net, outgoing, incoming, rest=None):
        self.net, self.outgoing, self.incoming, self.rest = net, outgoing, incoming, rest
        self.slot = net.recv_slots(net.n if rest is None else 1)

    def start(self):
        net = self.net
        send = None if self.rest is None else net.send_slot()
        for d in range(1, net.n):
            to = net.peer(d)
            slot = self.slot + net.e if self.rest is None else self.slot
            net.push(self.outgoing(to), self.incoming(net.e), (to, net.t), slot, shared=send)
        if self.rest is not None:
            net.all_sent(self.rest, send)

    def arrive(self, d):
        source = self.net.peer(d)
        self.net.landed(self.incoming(source), self.slot + source)
        return source

    def finish(self):
        self.net.landed(self.rest, self.slot)


class Dispatch:
    def __init__(self, net, outgoing, incoming):
        self.net, self.outgoing, self.incoming = net, outgoing, incoming
        self.send = Exchange(
            net, lambda b: outgoing.at[b], lambda b: incoming.at[b, net.core, net.y]
        )
        self.slot_y = net.recv_slots(net.n)
        self.slot_core = net.recv_slots(1)

    def start(self):
        net = self.net
        self.send.start()
        self.incoming[net.e, net.core, net.y] = self.outgoing[net.e]

    def relay_y(self):
        net = self.net
        for d in range(net.n):
            b = net.e if d == 0 else self.send.arrive(d)
            part = self.incoming.at[b, net.core, net.y]
            net.push(part, part, net.across_y(), self.slot_y + b)

    def relay_core(self):
        net = self.net
        for d in range(net.n):
            b = net.peer(d)
            net.landed(self.incoming.at[b, net.core, 1 - net.y], self.slot_y + b)
        part = self.incoming.at[:, net.core]
        net.push(part, part, net.other_core(), self.slot_core)

    def finish(self):
        self.net.landed(self.incoming.at[:, 1 - self.net.core], self.slot_core)


class Swap:
    def __init__(self, net, out_buf, in_buf, partner):
        self.net, self.out_buf, self.in_buf, self.partner = net, out_buf, in_buf, partner
        self.slot = net.recv_slots(1)

    def start(self, value):
        self.out_buf[...] = value.astype(self.out_buf.dtype)
        self.send()

    def send(self):
        self.net.push(self.out_buf, self.in_buf, self.partner, self.slot)

    def other(self):
        self.net.landed(self.in_buf, self.slot)
        return self.in_buf[...].astype(F32)

    def both(self):
        return self.out_buf[...].astype(F32) + self.other()


class Share:
    def __init__(self, net, halves):
        self.net, self.halves = net, halves
        self.slot = net.recv_slots(1)

    def start(self, value):
        net = self.net
        self.halves[net.core] = value.astype(self.halves.dtype)
        part = self.halves.at[net.core]
        net.push(part, part, net.other_core(), self.slot)

    def finish(self):
        net = self.net
        net.landed(self.halves.at[1 - net.core], self.slot)
        return jnp.concatenate([self.halves[0], self.halves[1]], axis=1)


def silu_both(value):
    gate = jax.nn.sigmoid(value)
    return value * gate, gate * (1.0 + value * (1.0 - gate))


def norm_scale(value):
    return lax.rsqrt(jnp.mean(value * value, axis=1, keepdims=True) + EPSILON)


def norm_back(grad_normed, source, scale, gain):
    weighted = grad_normed * gain
    inner = jnp.mean(weighted * source, axis=1, keepdims=True)
    return scale * weighted - scale * scale * scale * source * inner


PLACES = ["tok", "cot", "routes", "lengths", "parents", "gain_a", "gain_b", "wq", "wk", "wv"]
PLACES += ["wo", "router", "sg", "su", "sd", "eg", "eu", "ed"]
RESULTS = ["out", "gtok", "dga", "dgb", "dwq", "dwk", "dwv", "dwo", "drouter"]
RESULTS += ["dsg", "dsu", "dsd", "deg", "deu", "ded"]


def scratch_shapes(s):
    n, local, half = s.n, s.local, s.half
    depth, hidden, shared, cap = s.depth, s.hidden, s.shared, s.cap
    micro, nz = s.micro, s.n // 2
    model, wide, stack, tree = 2 * half, 2 * s.width, s.heads * local, n * local
    part = cap // 4
    vm = pltpu.VMEM
    return dict(
        w_kv=vm((n, depth, wide), BF),
        w_qo=vm((n, depth, wide), BF),
        w_sh=vm((3, n, depth, shared), BF),
        ext_in=vm((n, 16, 128), BF),
        tok_all=vm((n, 2, 2, micro * local // 4, model), BF),
        cos_all=vm((n, micro * local, 128), F32),
        sin_all=vm((n, micro * local, 128), F32),
        kv=vm((micro, n, local, wide), BF),
        q_rows=vm((micro, stack, 256), BF),
        expo=vm((micro, stack, tree), F32),
        total=vm((micro, stack, 1), F32),
        mixed=vm((micro, local, 256), F32),
        mixed_low=vm((micro * local, wide), BF),
        choice_half=vm((micro, local, n * cap // 2), BF),
        choice_wide=vm((micro, local, n * 128), BF),
        res=vm((micro, local, model), F32),
        n_one=vm((micro * local, model), BF),
        n_two=vm((micro * local, model), BF),
        c_out=vm((micro, n, part, model), BF),
        c_in=vm((micro, n, 2, 2, part, model), BF),
        x_out=vm((micro, n, part, model), BF),
        x_in=vm((micro, n, 2, 2, part, model), BF),
        h_out=vm((micro, n, 16, 128), BF),
        h_in=vm((micro, n, 16, 128), BF),
        gate_col=vm((micro, n * cap, 1), F32),
        e_h=vm((micro, n * cap, hidden), BF),
        e_dg=vm((micro, n * cap, hidden), BF),
        e_du=vm((micro, n * cap, hidden), BF),
        y_core=vm((micro, n, cap, half), BF),
        g_core=vm((micro, n, cap, half), BF),
        y_in=vm((micro, n, cap // 2, half), BF),
        y_far=vm((micro, n, cap // 2, half), BF),
        g_in=vm((micro, n, cap // 2, half), BF),
        g_far=vm((micro, n, cap // 2, half), BF),
        d_out=vm((micro, n, 8, 128), F32),
        d_in=vm((micro, n, 8, 128), F32),
        d_tensor=vm((micro, 4, 8, 128), F32),
        core_a=vm((micro, 2, local, half), F32),
        core_b=vm((4, micro * local, half), BF),
        core_c=vm((micro, 2, local, half), F32),
        s_grads=vm((3, micro * local, shared), BF),
        s_own=vm((2, micro * local, half), F32),
        y_swap=vm((4, micro, 2, local, half), BF),
        share_a=vm((micro, 2, local, half), F32),
        share_b=vm((micro, 2, local, half), F32),
        share_c=vm((micro, 2, local, half), F32),
        share_out=vm((micro, 2, local, half), BF),
        kv_part=vm((micro, n, local, wide), BF),
        kv_fx=vm((micro, 2, nz, local // 2, wide), BF),
        kv_fz=vm((micro, 2, nz, local // 2, wide), BF),
        sh_part=vm((3, n, depth, shared), BF),
        sh_fx=vm((3, nz, depth, shared), BF),
        sh_fz=vm((3, nz + 1, depth, shared), BF),
        w_part=vm((2, n, depth, wide), BF),
        w_fx=vm((2, nz, depth, wide), BF),
        w_fz=vm((2, nz, depth, wide), BF),
        gains_out=vm((n, 16, 128), F32),
        gains_in=vm((n, 16, 128), F32),
        stage=vm((2, half, hidden), F32),
        stage_d=vm((hidden, half), F32),
        save_sems=pltpu.SemaphoreType.DMA((6,)),
        send_sems=pltpu.SemaphoreType.DMA((SENDS,)),
        recv_sems=pltpu.SemaphoreType.DMA((RECVS,)),
    )


SENDS = 182
RECVS = 251


def layer_kernel(s, names, *refs):
    r = types.SimpleNamespace(**dict(zip(names, refs)))
    n, local, width, half = s.n, s.local, s.width, s.half
    depth, hidden, shared, cap = s.depth, s.hidden, s.shared, s.cap
    micro, heads = s.micro, s.heads
    rows, model, tree, wide, stack = micro * local, 2 * half, n * local, 2 * width, heads * local
    part = cap // 4
    net = Net(n, r.send_sems, r.recv_sems)
    me, core, y = net.e, net.core, net.y
    ready = net.greet()
    micros = range(micro)
    my_half = pl.ds(pl.multiple_of(core * half, 128), half)
    other_half = pl.ds(pl.multiple_of((1 - core) * half, 128), half)

    def rows_of(m):
        return slice(m * local, (m + 1) * local)

    left = (iota((width, wide), 1) == iota((width, wide), 0)).astype(BF)
    right = (iota((width, wide), 1) == iota((width, wide), 0) + width).astype(BF)
    r.w_kv[me] = (dot(r.wk[...], left) + dot(r.wv[...], right)).astype(BF)
    r.tok_all[me] = r.tok[...].reshape(2, 2, rows // 4, model)
    r.w_qo[me] = (dot(r.wq[...], left) + dot_tn(r.wo[...], right)).astype(BF)
    ext = [r.gain_a[...].astype(F32), r.gain_b[...].astype(F32), jnp.zeros((6, depth), F32)]
    ext = jnp.concatenate(ext + [r.router[...].astype(F32)], axis=0).astype(BF)
    pad = (iota((depth, 128), 1) == iota((depth, 128), 0)).astype(BF)
    r.ext_in[me] = dot(ext, pad).astype(BF)
    for i, name in enumerate(("sg", "su", "sd")):
        r.w_sh[i, me] = getattr(r, name)[...]

    slot_ty, slot_tc = net.recv_slots(n), net.recv_slots(n)

    def token_on(b, when):
        quarter = r.tok_all.at[b, core, y]
        net.push(quarter, quarter, net.across_y(), slot_ty + b, when)

    get_kv = Gather(net, lambda b, k: r.w_kv.at[b])
    get_qo = Gather(net, lambda b, k: r.w_qo.at[b])
    get_tok = Gather(net, lambda b, k: r.tok_all.at[b, core, y], on_land=token_on)
    get_sh = [Gather(net, lambda b, k, i=i: r.w_sh.at[i, b]) for i in range(3)]
    get_ext = Exchange(net, lambda b: r.ext_in.at[me], lambda b: r.ext_in.at[b], r.ext_in.at[0 : n - 1])
    ready()
    get_ext.start()
    get_kv.start()
    get_tok.start()
    get_qo.start()

    eye = (iota((128, 128), 0) == iota((128, 128), 1)).astype(BF)
    routes = dot_nt(eye, r.routes[...].astype(BF))
    lane = iota((local, 16), 1) - 8
    earlier = (iota((local, local), 1) < iota((local, local), 0)).astype(BF)

    def spread(span):
        of_lane = iota((16, n * span), 1) // span
        return (iota((16, n * span), 0) - 8 == of_lane).astype(BF)

    hot_one, hot_two, quarter = [], [], []
    send_c = [Dispatch(net, r.c_out.at[m], r.c_in.at[m]) for m in micros]
    send_h = [
        Exchange(
            net,
            lambda b, m=m: r.h_out.at[m, b],
            lambda b, m=m: r.h_in.at[m, b],
            r.h_in.at[m, 0 : n - 1],
        )
        for m in micros
    ]
    for m in micros:
        one = lane == routes[:, 2 * m : 2 * m + 1].astype(jnp.int32)
        two = lane == routes[:, 2 * m + 1 : 2 * m + 2].astype(jnp.int32)
        hot_one.append(one)
        hot_two.append(two)
        hits = (one | two).astype(F32)
        rank = jnp.where(hits > 0.5, dot(earlier, hits.astype(BF)), -1.0).astype(BF)

        def taken(span, first=0):
            wanted = iota((local, n * span), 1) % span + first
            return (dot(rank, spread(span)) == wanted.astype(F32)).astype(BF)

        r.choice_half[m] = taken(cap // 2, y * (cap // 2))
        r.choice_wide[m] = taken(128)
        quarter.append(taken(part, (core * 2 + y) * part))
        hit_rows = dot_tn(hits.astype(BF), r.choice_wide[m]).astype(BF)
        for b in range(n):
            r.h_out[m, b] = hit_rows[:, b * 128 : (b + 1) * 128]
        r.h_in[m, me] = r.h_out[m, me]
        picked = dot_tn(quarter[m], r.cot[rows_of(m)]).astype(BF)
        r.c_out[m] = picked.reshape(n, part, model)

    def segments(m):
        starts, ends, paths, shifts, begin = [], [], [], [], 0
        for seg in range(s.segs):
            size = r.lengths[m, seg]
            starts.append(begin)
            ends.append(begin + size)
            begin = begin + size
            if seg == 0:
                paths.append(jnp.int32(1))
                shifts.append(jnp.int32(0))
            else:
                parent = r.parents[m, seg]
                path, shift = jnp.int32(0), jnp.int32(0)
                for other in range(seg):
                    is_parent = parent == other
                    path = jnp.where(is_parent, paths[other], path)
                    shift = jnp.where(
                        is_parent, shifts[other] + ends[other] - starts[other], shift
                    )
                paths.append(path + (1 << seg))
                shifts.append(shift)
        return starts, ends, paths, shifts

    tables = [segments(m) for m in micros]

    def row_values(m, ids):
        starts, ends, paths, shifts = tables[m]
        path, place, own = jnp.zeros_like(ids), jnp.zeros_like(ids), jnp.zeros_like(ids)
        for seg in range(s.segs):
            inside = (ids >= starts[seg]) & (ids < ends[seg])
            path = jnp.where(inside, paths[seg], path)
            place = jnp.where(inside, ids - starts[seg] + shifts[seg], place)
            own = jnp.where(inside, 1 << seg, own)
        return path, place, own

    turn = (iota((1, 128), 1) % (HEAD // 2)).astype(F32)
    frequency = jnp.exp(turn * (-math.log(ROPE_BASE) / (HEAD // 2)))

    def angle_step(b, carry):
        ids = b * local + iota((local, 1), 0)
        place = jnp.concatenate([row_values(m, ids)[1] for m in micros], axis=0)
        angle = place.astype(F32) * frequency
        r.cos_all[b] = jnp.cos(angle)
        r.sin_all[b] = jnp.sin(angle)
        return carry

    lax.fori_loop(0, n, angle_step, 0)
    is_left = iota((1, wide), 1) < width
    swap_r, swap_c = iota((wide, wide), 0), iota((wide, wide), 1)
    lower = swap_c % HEAD < HEAD // 2
    swap = jnp.where(lower & (swap_r == swap_c + HEAD // 2), -1.0, 0.0)
    swap = jnp.where(~lower & (swap_r == swap_c - HEAD // 2), 1.0, swap)
    swap = jnp.where(is_left, swap, 0.0)
    swap_low = swap.astype(BF)

    def turns(b):
        cosine = jnp.concatenate([r.cos_all[b]] * (wide // 128), axis=1)
        sine = jnp.concatenate([r.sin_all[b]] * (wide // 128), axis=1)
        return jnp.where(is_left, cosine, 1.0), sine

    for distance in range(1, net.nz):
        get_kv.step(distance)
        get_tok.step(distance)
        get_qo.step(distance)
    get_ext.finish()
    high = net.z // 2
    near = [net.z + 1 - 2 * (net.z % 2), 2 - high, 3 - 3 * high]
    column = [zz * 2 + net.x for zz in near]
    across = [zz * 2 + 1 - net.x for zz in [net.z] + near]

    def token_core(b):
        net.landed(r.tok_all.at[b, core, 1 - y], slot_ty + b)
        both = r.tok_all.at[b, core]
        net.push(both, both, net.other_core(), slot_tc + b)

    for b in column:
        token_core(b)

    def lay(b):
        place = iota((128, model), 0)
        return (place < depth) & (place + b * depth == iota((128, model), 1))

    ext_all = jnp.zeros((16, model), F32)
    for b in range(n):
        ext_all = ext_all + dot(r.ext_in[b], lay(b).astype(BF))
    gain_one, gain_two = ext_all[0:1], ext_all[1:2]
    ext_low = ext_all.astype(BF)
    get_kv.finish()
    w_kv = r.w_kv[...].reshape(model, wide)
    w_kv_swapped = dot(w_kv, swap_low[:, :256]).astype(BF)

    def normed(block):
        value = block.astype(F32)
        return (value * norm_scale(value) * gain_one).astype(BF)

    def key_value(b):
        block = normed(r.tok_all[b].reshape(rows, model))
        cosine, sine = turns(b)
        swapped = dot(block, w_kv_swapped) * sine[:, :256]
        swapped = jnp.concatenate([swapped, jnp.zeros((rows, wide - 256), F32)], axis=1)
        both = (dot(block, w_kv) * cosine + swapped).astype(BF)
        for m in micros:
            r.kv[m, b] = both[rows_of(m)]

    for g in get_sh:
        g.start()
    key_value(me)

    def key_values_of(blocks):
        def step(i, carry):
            b = sum([(i == k).astype(jnp.int32) * one for k, one in enumerate(blocks)])
            net.landed(r.tok_all.at[b, 1 - core], slot_tc + b)
            key_value(b)
            return carry

        lax.fori_loop(0, len(blocks), step, 0)

    for b in across[:2]:
        get_tok.land(b)
    key_values_of(column)
    for b in across[2:]:
        get_tok.land(b)
    for b in across[:2]:
        token_core(b)
    key_values_of(across[:2])
    for b in across[2:]:
        token_core(b)
    get_qo.finish()
    for g in get_sh:
        g.step(1)
    key_values_of(across[2:])
    r.n_one[...] = normed(r.tok[...])
    w_qo = r.w_qo[...].reshape(model, wide)
    cosine, sine = turns(me)
    cosine = jnp.where(is_left, cosine, 0.0)
    queries = dot(r.n_one[...], w_qo) * cosine
    queries = queries + dot(r.n_one[...], dot(w_qo, swap_low).astype(BF)) * sine
    queries = queries.astype(BF)
    for m in micros:
        send_c[m].start()
        send_h[m].start()

    first, last = slice(0, 256), slice(wide - 256, wide)
    head_of = iota((1, 256), 1) // HEAD
    q_masks = [head_of == h for h in range(heads)]
    v_masks = [head_of == heads + h - (wide - 256) // HEAD for h in range(heads)]
    blank = jnp.zeros((local, wide - 256), F32)

    def by_head(block, masks):
        return jnp.concatenate(
            [jnp.where(mask, block, jnp.zeros_like(block)) for mask in masks], axis=0
        )

    def join_heads(value, masks):
        total = jnp.zeros((local, 256), F32)
        for h, mask in enumerate(masks):
            total = total + jnp.where(mask, value[h * local : (h + 1) * local], 0.0)
        return total

    def o_half(h):
        return r.w_qo[pl.ds(h * (n // 2), n // 2)].reshape(half, wide)

    core_a = [Swap(net, r.core_a.at[m, 0], r.core_a.at[m, 1], net.other_core()) for m in micros]
    core_c = [Swap(net, r.core_c.at[m, 0], r.core_c.at[m, 1], net.other_core()) for m in micros]
    core_b = [
        Swap(net, r.core_b.at[2 * i], r.core_b.at[2 * i + 1], net.other_core()) for i in range(2)
    ]
    y_swap = [
        [Swap(net, r.y_swap.at[i, m, 0], r.y_swap.at[i, m, 1], net.across_y()) for m in micros]
        for i in range(4)
    ]
    share_a = [Share(net, r.share_a.at[m]) for m in micros]
    share_b = [Share(net, r.share_b.at[m]) for m in micros]
    share_c = [Share(net, r.share_c.at[m]) for m in micros]
    share_out = [Share(net, r.share_out.at[m]) for m in micros]

    score_scale = HEAD**-0.5
    for m in micros:
        r.q_rows[m] = by_head(queries[rows_of(m)][:, first], q_masks)
        key_rows = r.kv[m, :, :, first].reshape(tree, 256)
        value_rows = r.kv[m, :, :, last].reshape(tree, 256)
        ids = me * local + iota((stack, 1), 0) % local
        path, unused, unused_two = row_values(m, ids)
        key_ids = iota((1, tree), 1)
        unused, unused_two, key_seg = row_values(m, key_ids)
        seen = ((path & key_seg) != 0) & (key_ids <= ids)
        scores = dot_nt(r.q_rows[m], key_rows) * score_scale
        expo = jnp.where(seen, jnp.exp(scores), 0.0)
        r.expo[m] = expo
        total = jnp.sum(expo, axis=1, keepdims=True)
        r.total[m] = total
        mixed = join_heads(dot(expo.astype(BF), value_rows) / total, v_masks)
        r.mixed[m] = mixed
        r.mixed_low[rows_of(m)] = jnp.concatenate([blank, mixed], axis=1).astype(BF)
        core_a[m].start(dot_nt(r.mixed_low[rows_of(m)], o_half(1 - core)))
    for g in get_sh:
        g.step(2)
    for m in micros:
        mine = dot_nt(r.mixed_low[rows_of(m)], o_half(core))
        y_swap[0][m].start(mine + core_a[m].other())
    for m in micros:
        share_a[m].start(y_swap[0][m].both())

    send_x = [Dispatch(net, r.x_out.at[m], r.x_in.at[m]) for m in micros]
    scale_two = []
    for m in micros:
        res = r.tok[rows_of(m)].astype(F32) + share_a[m].finish()
        r.res[m] = res
        scale_two.append(norm_scale(res))
        normed_two = (res * scale_two[m] * gain_two).astype(BF)
        r.n_two[rows_of(m)] = normed_two
        r.x_out[m] = dot_tn(quarter[m], normed_two).astype(BF).reshape(n, part, model)
        send_x[m].start()

    for g in get_sh:
        g.step(3)
    for m in micros:
        send_c[m].relay_y()
    gates = []
    for m in micros:
        logits = dot_nt(r.n_two[rows_of(m)], ext_low)
        z_one = jnp.sum(jnp.where(hot_one[m], logits, 0.0), axis=1, keepdims=True)
        z_two = jnp.sum(jnp.where(hot_two[m], logits, 0.0), axis=1, keepdims=True)
        z_top = jnp.maximum(z_one, z_two)
        e_one, e_two = jnp.exp(z_one - z_top), jnp.exp(z_two - z_top)
        chosen = jnp.where(hot_one[m], e_one, jnp.where(hot_two[m], e_two, 0.0))
        gates.append(chosen / (e_one + e_two))

    for m in micros:
        send_x[m].relay_y()
    for g in get_sh:
        g.finish()

    def wide_half(i, h):
        return r.w_sh[i, pl.ds(h * (n // 2), n // 2)].reshape(half, shared)

    def shared_step(m, carry):
        here = pl.ds(pl.multiple_of(m * local, local), local)
        normed_two = r.n_two[here]
        shared_g = dot(normed_two, r.w_sh[0].reshape(model, shared))
        shared_u = dot(normed_two, r.w_sh[1].reshape(model, shared))
        act, slope = silu_both(shared_g)
        shared_h = (act * shared_u).astype(BF)
        grad_h = dot(r.cot[here], r.w_sh[2].reshape(model, shared))
        grad_g = (grad_h * shared_u * slope).astype(BF)
        grad_u = (grad_h * act).astype(BF)
        r.s_grads[0, here] = grad_g
        r.s_grads[1, here] = grad_u
        r.s_grads[2, here] = shared_h
        other, own = 1 - core, core
        back = dot_nt(grad_g, wide_half(0, other)) + dot_nt(grad_u, wide_half(1, other))
        r.core_b[0, here] = back.astype(BF)
        r.core_b[2, here] = dot_nt(shared_h, wide_half(2, other)).astype(BF)
        back = dot_nt(grad_g, wide_half(0, own)) + dot_nt(grad_u, wide_half(1, own))
        r.s_own[0, here] = back
        r.s_own[1, here] = dot_nt(shared_h, wide_half(2, own))
        return carry

    lax.fori_loop(0, micro, shared_step, 0)
    for swap_b in core_b:
        swap_b.send()
    for i, (rows_a, rows_b) in enumerate(((r.n_two, 0), (r.n_two, 1), (r.cot, 2))):
        grads = dot_tn(rows_a[...], r.s_grads[rows_b])
        r.sh_part[i] = grads.astype(BF).reshape(n, depth, shared)
    sum_sh = [
        Chain(net, lambda b, i=i: r.sh_part.at[i, b], r.sh_fx.at[i], r.sh_fz.at[i])
        for i in range(3)
    ]

    for m in micros:
        send_c[m].relay_core()
    for m in micros:
        send_x[m].relay_core()
    for m in micros:
        send_h[m].finish()
        send_c[m].finish()

    slot_gc = net.recv_slots(micro)
    slot_yc = net.recv_slots(micro)
    slot_yy = net.recv_slots(micro)
    slot_gy = net.recv_slots(micro)
    my_slots = pl.ds(pl.multiple_of(y * (cap // 2), cap // 2), cap // 2)
    far_slots = pl.ds(pl.multiple_of((1 - y) * (cap // 2), cap // 2), cap // 2)
    send_g = [
        Exchange(
            net,
            lambda b, m=m: r.g_core.at[m, b, my_slots],
            lambda b, m=m: r.g_in.at[m, b],
            r.g_in.at[m, 0 : n - 1],
        )
        for m in micros
    ]
    send_y = [
        Exchange(
            net,
            lambda b, m=m: r.y_core.at[m, b, my_slots],
            lambda b, m=m: r.y_in.at[m, b],
            r.y_in.at[m, 0 : n - 1],
        )
        for m in micros
    ]
    send_d = [
        Exchange(
            net,
            lambda b, m=m: r.d_out.at[m, b],
            lambda b, m=m: r.d_in.at[m, b],
            r.d_in.at[m, 0 : n - 1],
        )
        for m in micros
    ]
    slot_eye = eye[:cap]
    slot_line = iota((cap, 128), 0) == iota((cap, 128), 1)
    own_lane = iota((n * cap, 16), 1) - 8 == me
    group = 4
    halves = [slice(0, half), slice(half, model)]

    def expert_gates(m):
        x_rows = r.x_in[m].reshape(n * cap, model)
        z_all = dot_nt(x_rows, ext_low)
        hit = jnp.concatenate([dot_nt(slot_eye, r.h_in[m, b]) for b in range(n)], axis=0)
        z_own = jnp.sum(jnp.where(own_lane, z_all, 0.0), axis=1, keepdims=True)
        z_other = jnp.sum(jnp.where(own_lane, 0.0, z_all * hit), axis=1, keepdims=True)
        z_top = jnp.maximum(z_own, z_other)
        e_own, e_other = jnp.exp(z_own - z_top), jnp.exp(z_other - z_top)
        r.gate_col[m] = e_own / (e_own + e_other)

    def expert_rows(m, i):
        count = group * cap
        span = slice(i * group, (i + 1) * group)
        flat = slice(i * count, (i + 1) * count)
        x = r.x_in[m, span].reshape(count, model)
        c = r.c_in[m, span].reshape(count, model)
        gate = r.gate_col[m, flat]
        gate_pre = dot(x, r.eg[...])
        up_pre = dot(x, r.eu[...])
        act, slope = silu_both(gate_pre)
        hid = (act * up_pre).astype(BF)
        grad_y = (gate * c.astype(F32)).astype(BF)
        grad_hid = dot_nt(grad_y, r.ed[...])
        grad_g = (grad_hid * up_pre * slope).astype(BF)
        grad_u = (grad_hid * act).astype(BF)
        r.e_h[m, flat] = hid
        r.e_dg[m, flat] = grad_g
        r.e_du[m, flat] = grad_u
        dots = jnp.zeros((count, 1), F32)
        for cut in halves:
            out = dot(hid, r.ed[:, cut])
            r.tok_all[span, 0, m, :, cut] = out.astype(BF).reshape(group, cap, half)
            dots = dots + jnp.sum(out * c[:, cut].astype(F32), axis=1, keepdims=True)
            back = dot_nt(grad_g, r.eg[cut]) + dot_nt(grad_u, r.eu[cut])
            r.tok_all[span, 1, m, :, cut] = back.astype(BF).reshape(group, cap, half)
        r.c_in[m, span] = grad_y.reshape(group, 2, 2, part, model)
        for b in range(group):
            line = jnp.where(slot_line, dots[b * cap : (b + 1) * cap], 0.0)
            line = jnp.sum(line, axis=0, keepdims=True)
            r.d_out[m, i * group + b] = jnp.broadcast_to(line, (8, 128))

    def expert_sent(m):
        net.push(r.tok_all.at[:, 1, m, :, other_half], r.g_core.at[m], net.other_core(), slot_gc + m)
        net.push(r.tok_all.at[:, 0, m, :, other_half], r.y_core.at[m], net.other_core(), slot_yc + m)

    def add_g(m):
        net.landed(r.g_core.at[m], slot_gc + m)
        mine = r.tok_all[:, 1, m, :, my_half].astype(F32)
        r.g_core[m] = (mine + r.g_core[m].astype(F32)).astype(BF)
        net.push(r.g_core.at[m, :, far_slots], r.g_far.at[m], net.across_y(), slot_gy + m)

    def return_g(m):
        net.landed(r.g_far.at[m], slot_gy + m)
        both = r.g_core[m, :, my_slots].astype(F32) + r.g_far[m].astype(F32)
        r.g_core[m, :, my_slots] = both.astype(BF)
        send_g[m].start()
        send_d[m].start()
        r.g_in[m, me] = r.g_core[m, me, my_slots]
        r.d_in[m, me] = r.d_out[m, me]

    def add_y(m):
        net.landed(r.y_core.at[m], slot_yc + m)
        mine = r.tok_all[:, 0, m, :, my_half].astype(F32)
        r.y_core[m] = (mine + r.y_core[m].astype(F32)).astype(BF)
        net.push(r.y_core.at[m, :, far_slots], r.y_far.at[m], net.across_y(), slot_yy + m)

    def return_y(m):
        net.landed(r.y_far.at[m], slot_yy + m)
        both = r.y_core[m, :, my_slots].astype(F32) + r.y_far[m].astype(F32)
        r.y_core[m, :, my_slots] = both.astype(BF)
        send_y[m].start()
        r.y_in[m, me] = r.y_core[m, me, my_slots]

    saves = []

    def all_slots(ref, cut):
        return ref[..., cut].reshape(micro * n * cap, -1)

    def save(source, target, i):
        copy = pltpu.make_async_copy(source, target, r.save_sems.at[i])
        copy.start()
        saves.append(copy)

    def weight_grads(i):
        whole = slice(None)
        if i < 2:
            grads, target = ((r.e_dg, r.deg), (r.e_du, r.deu))[i]
            for h, cut in enumerate(halves):
                if i == 1:
                    saves[h].wait()
                r.stage[h] = dot_tn(all_slots(r.x_in, cut), all_slots(grads, whole))
                save(r.stage.at[h], target.at[cut], 2 * i + h)
        else:
            for h, cut in enumerate(halves):
                if h == 1:
                    saves[4].wait()
                r.stage_d[...] = dot_tn(all_slots(r.e_h, whole), all_slots(r.c_in, cut))
                save(r.stage_d, r.ded.at[:, cut], 4 + h)

    net.drain()
    sum_sh[0].start()
    sum_sh[1].start()
    for m in micros:
        send_x[m].finish()
        if m > 0:
            sum_sh[0].step(3)
        expert_gates(m)
        for i in range(n // group):
            if m > 0 and i == 1:
                add_g(m - 1)
                sum_sh[0].step(2)
            expert_rows(m, i)
        expert_sent(m)
    return_g(0)
    sum_sh[0].step(1)
    weight_grads(0)
    add_g(1)
    weight_grads(1)
    return_g(1)
    sum_sh[2].start()
    sum_sh[1].step(3)
    weight_grads(2)
    sum_sh[1].step(2)

    for m in micros:
        add_y(m)
    d_core = [Swap(net, r.d_tensor.at[m, 0], r.d_tensor.at[m, 1], net.other_core()) for m in micros]
    d_y = [Swap(net, r.d_tensor.at[m, 2], r.d_tensor.at[m, 3], net.across_y()) for m in micros]
    eight = iota((8, 128), 0)
    d_rows = []
    for m in micros:
        send_d[m].finish()
        line = jnp.zeros((8, 128), F32)
        for b in range(n):
            line = line + jnp.where(eight == b, r.d_in[m, b], 0.0)
        d_rows.append(line)
        d_core[m].start(line)
    shared_grad = r.s_own[0] + core_b[0].other()
    for m in micros:
        d_y[m].start(d_rows[m] + d_core[m].other())
    for m in micros:
        send_g[m].finish()
        moe_grad = dot(r.choice_half[m], r.g_in[m].reshape(n * cap // 2, half))
        y_swap[1][m].start(moe_grad + shared_grad[rows_of(m)])
    net.drain(bulk=False)
    sum_sh[1].step(1)
    grad_logits = []
    for m in micros:
        d_all = d_y[m].both()
        grad_gate = jnp.zeros((local, 16), F32)
        for b in range(n):
            picked = r.choice_wide[m, :, b * 128 : (b + 1) * 128].astype(F32) * d_all[b : b + 1]
            grad_gate = jnp.where(lane == b, jnp.sum(picked, axis=1, keepdims=True), grad_gate)
        inner = jnp.sum(gates[m] * grad_gate, axis=1, keepdims=True)
        grad_logits.append((gates[m] * (grad_gate - inner)).astype(BF))
        share_b[m].start(y_swap[1][m].both())


    kv_sums, grad_queries, gain_rows = [], [], []
    for m in micros:
        grad_two = share_b[m].finish() + dot(grad_logits[m], ext_low)
        res = r.res[m]
        cot = r.cot[rows_of(m)].astype(F32)
        grad_res = cot + norm_back(grad_two, res, scale_two[m], gain_two)
        r.gtok[rows_of(m)] = grad_res
        gain_rows.append(jnp.sum(grad_two * res * scale_two[m], axis=0, keepdims=True))
        key_rows = r.kv[m, :, :, first].reshape(tree, 256)
        value_rows = r.kv[m, :, :, last].reshape(tree, 256)
        total = r.total[m]
        gm = by_head(dot(grad_res.astype(BF), r.w_qo[:, :, last].reshape(model, 256)), v_masks)
        mixed = jnp.concatenate([r.mixed[m]] * heads, axis=0)
        delta = jnp.sum(gm * mixed, axis=1, keepdims=True) / total
        grad_summed = (gm / total).astype(BF)
        expo = r.expo[m]
        ds = (expo * (dot_nt(grad_summed, value_rows) - delta)).astype(BF)
        grad_k = dot_tn(ds, r.q_rows[m]) * score_scale
        grad_v = dot_tn(expo.astype(BF), grad_summed)
        over = 512 - wide
        middle = grad_k[:, 256 - over :] + grad_v[:, :over]
        grad_kv = jnp.concatenate([grad_k[:, : 256 - over], middle, grad_v[:, over:]], axis=1)
        r.kv_part[m] = grad_kv.astype(BF).reshape(n, local, wide)
        for k in range(2):
            span = slice(k * (local // 2), (k + 1) * (local // 2))
            one = Scatter(
                net,
                lambda b, m=m, span=span: r.kv_part.at[m, b, span],
                r.kv_fx.at[m, k],
                r.kv_fz.at[m, k],
            )
            one.start()
            kv_sums.append(one)
        if m == 0:
            for k in micros:
                return_y(k)
        grad_query = join_heads(dot(ds, key_rows), q_masks) * score_scale
        grad_queries.append(jnp.concatenate([grad_query, blank], axis=1))

    cosine, sine = turns(me)

    def turned_back(grad):
        return (grad * cosine - dot(grad, swap, EXACT) * sine).astype(BF)

    for one in kv_sums:
        one.forward()
    sum_sh[2].step(3)
    grad_q = turned_back(jnp.concatenate(grad_queries, axis=0))
    grad_attn = r.gtok[...].astype(BF)
    part_qo = dot_tn(r.n_one[...], grad_q) + dot_tn(grad_attn, r.mixed_low[...])
    r.w_part[0] = part_qo.astype(BF).reshape(n, depth, wide)
    sum_w = [
        Scatter(net, lambda b, i=i: r.w_part.at[i, b], r.w_fx.at[i], r.w_fz.at[i])
        for i in range(2)
    ]
    sum_w[0].start()

    shared_y = r.s_own[1] + core_b[1].other()
    for m in micros:
        send_y[m].finish()
        gate_wide = dot(gates[m], spread(cap // 2).astype(F32), EXACT)
        gate_high = gate_wide.astype(BF).astype(F32)
        pick = r.choice_half[m].astype(F32)
        y_rows = r.y_in[m].reshape(n * cap // 2, half)
        moe_y = dot((pick * gate_high).astype(BF), y_rows)
        moe_y = moe_y + dot((pick * (gate_wide - gate_high)).astype(BF), y_rows)
        y_swap[2][m].start(moe_y + shared_y[rows_of(m)])
    sum_sh[2].step(2)

    def weight_half(ref, h):
        return ref[pl.ds(h * (n // 2), n // 2)].reshape(half, wide)

    grad_kvs = []
    for m in micros:
        total = jnp.concatenate([one.finish() for one in kv_sums[2 * m : 2 * m + 2]], axis=0)
        cos_m, sin_m = cosine[rows_of(m)], sine[rows_of(m)]
        grad_kv = (total * cos_m - dot(total, swap, EXACT) * sin_m).astype(BF)
        grad_kvs.append(grad_kv)
        q_m = grad_q[rows_of(m)]
        other = dot_nt(q_m, weight_half(r.w_qo, 1 - core))
        core_c[m].start(other + dot_nt(grad_kv, weight_half(r.w_kv, 1 - core)))
    for m in micros:
        mine = dot_nt(grad_q[rows_of(m)], weight_half(r.w_qo, core))
        mine = mine + dot_nt(grad_kvs[m], weight_half(r.w_kv, core))
        y_swap[3][m].start(mine + core_c[m].other())
    part_kv = dot_tn(r.n_one[...], jnp.concatenate(grad_kvs, axis=0))
    r.w_part[1] = part_kv.astype(BF).reshape(n, depth, wide)
    sum_w[1].start()
    sum_w[0].forward()
    sum_sh[2].step(1)
    for m in micros:
        share_c[m].start(y_swap[3][m].both())
    for m in micros:
        res_half = jnp.where(core == 0, r.res[m, :, :half], r.res[m, :, half:])
        share_out[m].start(res_half + y_swap[2][m].both())
    sum_w[1].forward()

    gain_one_row = jnp.zeros((1, model), F32)
    for m in micros:
        grad_one = share_c[m].finish()
        tok = r.tok[rows_of(m)].astype(F32)
        scale_one = norm_scale(tok)
        r.gtok[rows_of(m)] += norm_back(grad_one, tok, scale_one, gain_one)
        gain_one_row = gain_one_row + jnp.sum(grad_one * tok * scale_one, axis=0, keepdims=True)
    grad_router = jnp.zeros((16, model), F32)
    for m in micros:
        grad_router = grad_router + dot_tn(grad_logits[m], r.n_two[rows_of(m)])
    line = iota((16, model), 0)
    small = jnp.where(line == 0, gain_one_row, grad_router)
    small = jnp.where(line == 1, gain_rows[0] + gain_rows[1], small)
    high_part = small.astype(BF)
    low_part = (small - high_part.astype(F32)).astype(BF)
    for b in range(n):
        place = lay(b).astype(BF)
        r.gains_out[b] = dot_nt(high_part, place) + dot_nt(low_part, place)
    send_gains = Exchange(
        net, lambda b: r.gains_out.at[b], lambda b: r.gains_in.at[b], r.gains_in.at[0 : n - 1]
    )
    send_gains.start()
    r.gains_in[me] = r.gains_out[me]
    for m in micros:
        r.out[rows_of(m)] = share_out[m].finish()

    qo = sum_w[0].finish()
    r.dwq[...] = qo[:, :width]
    depth_eye = (iota((depth, depth), 0) == iota((depth, depth), 1)).astype(F32)
    r.dwo[...] = dot_tn(qo[:, width:], depth_eye, EXACT)
    kv = sum_w[1].finish()
    r.dwk[...] = kv[:, :width]
    r.dwv[...] = kv[:, width:]
    for i, target in enumerate((r.dsg, r.dsu, r.dsd)):
        sum_sh[i].finish(target)
    send_gains.finish()
    gains = jnp.zeros((16, 128), F32)
    for b in range(n):
        gains = gains + r.gains_in[b]
    r.dga[...] = gains[0:1, :depth]
    r.dgb[...] = gains[1:2, :depth]
    r.drouter[...] = gains[8:16, :depth]
    for copy in saves[2:4] + saves[5:]:
        copy.wait()
    net.drain()


def settle_kernel(count, *refs):
    sources, targets, stops = refs[:count], refs[count : 2 * count], refs[2 * count : 3 * count]
    sems = refs[3 * count]
    reads = [
        pltpu.make_async_copy(a, b, sems.at[0, i]) for i, (a, b) in enumerate(zip(sources, stops))
    ]
    writes = [
        pltpu.make_async_copy(a, b, sems.at[1, i]) for i, (a, b) in enumerate(zip(stops, targets))
    ]
    for read in reads:
        read.start()
    for read, write in zip(reads, writes):
        read.wait()
        write.start()
    for write in writes:
        write.wait()


def fits(mesh):
    return mesh.shape["expert"] == 8 and mesh.shape["tensor"] == 4


def fused_body(
    tokens,
    out_grad,
    routes,
    lengths,
    parents,
    attn_gain,
    ffn_gain,
    w_query,
    w_key,
    w_value,
    w_out,
    router,
    shared_gate,
    shared_up,
    shared_down,
    expert_gate,
    expert_up,
    expert_down,
):
    micro, local, model = tokens.shape
    n = lax.axis_size("expert")
    experts = router.shape[1]
    depth, width = w_query.shape
    hidden, shared = expert_gate.shape[2], shared_gate.shape[1]
    s = types.SimpleNamespace(
        n=n,
        micro=micro,
        local=local,
        half=model // 2,
        depth=depth,
        width=width,
        heads=width // HEAD,
        hidden=hidden,
        shared=shared,
        cap=4 * local // experts,
        segs=lengths.shape[1],
    )
    rows = micro * local
    scratch = scratch_shapes(s)
    names = PLACES + RESULTS + list(scratch)
    shape = jax.ShapeDtypeStruct
    vmem, smem = pl.BlockSpec(memory_space=pltpu.VMEM), pl.BlockSpec(memory_space=pltpu.SMEM)
    hbm = pl.BlockSpec(memory_space=pl.ANY)
    results = (
        shape((rows, model), BF),
        shape((rows, model), F32),
        shape((1, depth), F32),
        shape((1, depth), F32),
        shape((depth, width), F32),
        shape((depth, width), F32),
        shape((depth, width), F32),
        shape((width, depth), F32),
        shape((experts, depth), F32),
        shape((depth, shared), F32),
        shape((depth, shared), F32),
        shape((depth, shared), F32),
        shape((model, hidden), F32),
        shape((model, hidden), F32),
        shape((hidden, model), F32),
    )
    found = pl.pallas_call(
        functools.partial(layer_kernel, s, names),
        out_shape=results,
        in_specs=[vmem] * 3 + [smem] * 2 + [vmem] * 13,
        out_specs=[vmem] * 12 + [hbm] * 3,
        scratch_shapes=list(scratch.values()),
        compiler_params=pltpu.CompilerParams(
            collective_id=0, has_side_effects=True, vmem_limit_bytes=VMEM_LIMIT
        ),
    )(
        tokens.reshape(rows, model),
        out_grad.reshape(rows, model),
        routes.transpose(0, 2, 1).reshape(2 * micro, local),
        lengths,
        parents,
        attn_gain.reshape(1, depth),
        ffn_gain.reshape(1, depth),
        w_query,
        w_key,
        w_value,
        w_out,
        router.T,
        shared_gate,
        shared_up,
        shared_down.T,
        expert_gate[0],
        expert_up[0],
        expert_down[0],
    )
    settled = pl.pallas_call(
        functools.partial(settle_kernel, len(results)),
        out_shape=results,
        in_specs=[hbm] * len(results),
        out_specs=[hbm] * len(results),
        scratch_shapes=[pltpu.VMEM(one.shape, one.dtype) for one in results]
        + [pltpu.SemaphoreType.DMA((2, len(results)))],
        compiler_params=pltpu.CompilerParams(vmem_limit_bytes=VMEM_LIMIT),
    )(*found)
    out, gtok, dga, dgb, dwq, dwk, dwv, dwo, drouter, dsg, dsu, dsd, deg, deu, ded = settled
    return (
        out.reshape(micro, local, model),
        gtok.reshape(micro, local, model),
        dga.reshape(depth),
        dgb.reshape(depth),
        dwq,
        dwk,
        dwv,
        dwo,
        drouter.T,
        dsg,
        dsu,
        dsd.T,
        deg[None],
        deu[None],
        ded[None],
    )


def solution(mesh):
    in_specs = (
        P(None, "expert", None),
        P(None, "expert", None),
        P(None, "expert", None),
        P(),
        P(),
        P("expert"),
        P("expert"),
        P("expert", "tensor"),
        P("expert", "tensor"),
        P("expert", "tensor"),
        P("tensor", "expert"),
        P("expert", None),
        P("expert", "tensor"),
        P("expert", "tensor"),
        P("tensor", "expert"),
        P("expert", None, "tensor"),
        P("expert", None, "tensor"),
        P("expert", "tensor", None),
    )
    out_specs = (
        P(None, "expert", None),
        P(None, "expert", None),
        P("expert"),
        P("expert"),
        P("expert", "tensor"),
        P("expert", "tensor"),
        P("expert", "tensor"),
        P("tensor", "expert"),
        P("expert", None),
        P("expert", "tensor"),
        P("expert", "tensor"),
        P("tensor", "expert"),
        P("expert", None, "tensor"),
        P("expert", None, "tensor"),
        P("expert", "tensor", None),
    )
    chosen = fused_body if fits(mesh) else plain_body
    return jax.shard_map(chosen, mesh=mesh, in_specs=in_specs, out_specs=out_specs, check_vma=False)
```

profile of v0, /device:TPU:0, one launch (start us, length us, event | category | flops | bytes accessed | tf_op | source)
XLA Modules:
  0.0 181.8 jit_solution(16206128651363071741)
XLA Ops:
  0.7 175.1 %shard_map.289 = (bf16[256,768]{1,0:T(8,128)(2,1)}, f32[256,768]{1,0:T(8,128)}, f32[1,96]{1,0:T(1,128)}, f32[1,96]{1,0:T(1,128)}, f32[96,192]{1,0:T(8,128)}, /*i...) custom-call(bf16[256,768]{1,0:T(8,128)(2,1)} %bitcast.24, ...), custom_call_target="tpu_custom_call" | custom-call | tf_op jit(solution)/shard_map/pallas_call | solution.py:1738
  175.8 5.8 %shard_map.290 = (bf16[256,768]{1,0:T(8,128)(2,1)}, f32[256,768]{1,0:T(8,128)}, f32[1,96]{1,0:T(1,128)}, f32[1,96]{1,0:T(1,128)}, f32[96,192]{1,0:T(8,128)}, /*i...) custom-call(bf16[256,768]{1,0:T(8,128)(2,1)} %get-tuple-element.45.r, ...), custom_call_target="tpu_custom_call" | custom-call | tf_op jit(solution)/shard_map/pallas_call | solution.py:1767
where the time goes:
time: 182 us
  Pallas kernels  181 us (99%)
    pallas_call x1, Pallas kernels, fused_body(): pl.pallas_call(functools.partial(layer_kernel, s, names), out_shape=resul...  175 us
    pallas_call x1, Pallas kernels, fused_body(): pl.pallas_call(functools.partial(settle_kernel, len(results)), out_shape=...  5.82 us

commit v1 on v0

--- a/solution.py
+++ b/solution.py
@@ -783,7 +783,7 @@
         self.send = Exchange(
             net, lambda b: outgoing.at[b], lambda b: incoming.at[b, net.core, net.y]
         )
-        self.slot_y = net.recv_slots(net.n)
+        self.slot_y = net.recv_slots(1)
         self.slot_core = net.recv_slots(1)
 
     def start(self):
@@ -796,13 +796,11 @@
         for d in range(net.n):
             b = net.e if d == 0 else self.send.arrive(d)
             part = self.incoming.at[b, net.core, net.y]
-            net.push(part, part, net.across_y(), self.slot_y + b)
+            net.push(part, part, net.across_y(), self.slot_y)
 
     def relay_core(self):
         net = self.net
-        for d in range(net.n):
-            b = net.peer(d)
-            net.landed(self.incoming.at[b, net.core, 1 - net.y], self.slot_y + b)
+        net.landed(self.incoming.at[:, net.core, 1 - net.y], self.slot_y)
         part = self.incoming.at[:, net.core]
         net.push(part, part, net.other_core(), self.slot_core)
 
@@ -863,7 +861,7 @@
 
 
 PLACES = ["tok", "cot", "routes", "lengths", "parents", "gain_a", "gain_b", "wq", "wk", "wv"]
-PLACES += ["wo", "router", "sg", "su", "sd", "eg", "eu", "ed"]
+PLACES += ["wo", "router", "sg", "su", "sd", "eg_far", "eu_far", "ed_far"]
 RESULTS = ["out", "gtok", "dga", "dgb", "dwq", "dwk", "dwv", "dwo", "drouter"]
 RESULTS += ["dsg", "dsu", "dsd", "deg", "deu", "ded"]
 
@@ -934,6 +932,10 @@
         w_fz=vm((2, nz, depth, wide), BF),
         gains_out=vm((n, 16, 128), F32),
         gains_in=vm((n, 16, 128), F32),
+        eg=vm((model, hidden), BF),
+        eu=vm((model, hidden), BF),
+        ed=vm((hidden, model), BF),
+        load_sems=pltpu.SemaphoreType.DMA((3,)),
         stage=vm((2, half, hidden), F32),
         stage_d=vm((hidden, half), F32),
         save_sems=pltpu.SemaphoreType.DMA((6,)),
@@ -943,7 +945,7 @@
 
 
 SENDS = 182
-RECVS = 251
+RECVS = 223
 
 
 def layer_kernel(s, names, *refs):
@@ -956,6 +958,10 @@
     net = Net(n, r.send_sems, r.recv_sems)
     me, core, y = net.e, net.core, net.y
     ready = net.greet()
+    loads = [
+        pltpu.make_async_copy(far, near, r.load_sems.at[i])
+        for i, (far, near) in enumerate(((r.eg_far, r.eg), (r.eu_far, r.eu), (r.ed_far, r.ed)))
+    ]
     micros = range(micro)
     my_half = pl.ds(pl.multiple_of(core * half, 128), half)
     other_half = pl.ds(pl.multiple_of((1 - core) * half, 128), half)
@@ -988,6 +994,8 @@
     get_ext = Exchange(net, lambda b: r.ext_in.at[me], lambda b: r.ext_in.at[b], r.ext_in.at[0 : n - 1])
     ready()
     get_ext.start()
+    for load in loads:
+        load.start()
     get_kv.start()
     get_tok.start()
     get_qo.start()
@@ -1450,6 +1458,8 @@
                 save(r.stage_d, r.ded.at[:, cut], 4 + h)
 
     net.drain()
+    for load in loads:
+        load.wait()
     sum_sh[0].start()
     sum_sh[1].start()
     for m in micros:
@@ -1738,7 +1748,7 @@
     found = pl.pallas_call(
         functools.partial(layer_kernel, s, names),
         out_shape=results,
-        in_specs=[vmem] * 3 + [smem] * 2 + [vmem] * 13,
+        in_specs=[vmem] * 3 + [smem] * 2 + [vmem] * 10 + [hbm] * 3,
         out_specs=[vmem] * 12 + [hbm] * 3,
         scratch_shapes=list(scratch.values()),
         compiler_params=pltpu.CompilerParams(

time: 182 us -> 181 us (level)
  no operation moved by 1% of the time
where the time goes in v1:
time: 181 us
  Pallas kernels  180 us (99%)
    pallas_call x1, Pallas kernels, fused_body(): pl.pallas_call(functools.partial(layer_kernel, s, names), out_shape=resul...  174 us
    pallas_call x1, Pallas kernels, fused_body(): pl.pallas_call(functools.partial(settle_kernel, len(results)), out_shape=...  5.82 us

profile of v1, /device:TPU:0, one launch (start us, length us, event | category | flops | bytes accessed | tf_op | source)
XLA Modules:
  0.0 180.9 jit_solution(6463367534319284668)
XLA Ops:
  0.7 174.2 %shard_map.289 = (bf16[256,768]{1,0:T(8,128)(2,1)}, f32[256,768]{1,0:T(8,128)}, f32[1,96]{1,0:T(1,128)}, f32[1,96]{1,0:T(1,128)}, f32[96,192]{1,0:T(8,128)}, /*i...) custom-call(bf16[256,768]{1,0:T(8,128)(2,1)} %bitcast.24, ...), custom_call_target="tpu_custom_call" | custom-call | tf_op jit(solution)/shard_map/pallas_call | solution.py:1748
  174.9 5.8 %shard_map.290 = (bf16[256,768]{1,0:T(8,128)(2,1)}, f32[256,768]{1,0:T(8,128)}, f32[1,96]{1,0:T(1,128)}, f32[1,96]{1,0:T(1,128)}, f32[96,192]{1,0:T(8,128)}, /*i...) custom-call(bf16[256,768]{1,0:T(8,128)(2,1)} %get-tuple-element.45.r, ...), custom_call_target="tpu_custom_call" | custom-call | tf_op jit(solution)/shard_map/pallas_call | solution.py:1777
